TPU v7x, 256 devices: a whole 4x4x8 slice. The times are simulated.
256 devices in a mesh: jgrp: 16 (over y, x), energy: 16 (over z, core).
Axes of the slice: x: 4, y: 4, z: 8, core: 2. Of those that a mesh axis runs over, the one named last changes fastest.
Arguments:
- s_real: bfloat16 [32, 256, 256, 256], P('jgrp', 'energy'), may hold values from -3 to 3
- s_imag: bfloat16 [32, 256, 256, 256], P('jgrp', 'energy'), may hold values from -3 to 3
- level_map: int32 [32, 256], P('jgrp'), may hold values from 0 to 511
- channel_count: int32 [32], P('jgrp'), may hold values from 1 to 256, as said below
- prefactor: float32 [512, 256], P(None, 'energy'), may hold values from 0.003 to 0.03
- maxwell: float32 [8, 256], P(None, 'energy'), may hold values from 0.000390625 to 0.00390625
Outputs:
- rates: float32 [512, 8, 512], P(('jgrp', 'energy'))
Inputs may be any that keep to these rules, and one draw needn't show every extreme that they name: `channel_count`: rises with J from about 256 / 4; the last block has exactly 256.
All inputs are finite; a program needn't handle non-finite values.
Results may differ from a plain program's by a relative error of at most 0.0003.
Values sent between devices are 32-bit elements; how exact they have to be, the bound alone decides.
No kernel may reach another device: no remote copies, remote signals or barrier semaphores. Data moves between devices by JAX's collectives and lax.ppermute only.
A program may use at most 128 MiB of HBM per device.

v0:
```python
import jax
import jax.numpy as jnp
from jax import lax
from jax.sharding import PartitionSpec as P


def body(s_real, s_imag, level_map, channel_count, prefactor, maxwell):
    j_local = s_real.shape[0]
    chans = s_real.shape[2]
    levels = prefactor.shape[0]
    jgroup = lax.axis_index("jgrp")
    chan = jnp.arange(chans, dtype=jnp.int32)
    eye = (chan[:, None] == chan[None, :]).astype(jnp.float32)
    level_ids = jnp.arange(levels, dtype=jnp.int32)
    blocks = []
    for block in range(j_local):
        factor = (2 * (jgroup * j_local + block) + 1).astype(jnp.float32)
        real_part = s_real[block].astype(jnp.float32)
        imag_part = s_imag[block].astype(jnp.float32)
        weighted = (((eye - real_part) ** 2 + imag_part**2) * factor).astype(jnp.bfloat16)
        segment = jnp.where(chan < channel_count[block], level_map[block], -1)
        columns = (segment[:, None] == level_ids[None, :]).astype(jnp.bfloat16)
        blocks.append((weighted, segment, columns))
    share = levels // lax.axis_size("jgrp")
    wanted = jnp.arange(share * lax.axis_size("jgrp"), dtype=jnp.int32)
    total = None
    for weighted, segment, columns in blocks:
        picks = (segment[None, :] == wanted[:, None]).astype(jnp.bfloat16)
        rowsum = jnp.einsum(
            "rc,ecd->erd", picks, weighted, preferred_element_type=jnp.float32
        ).astype(jnp.bfloat16)
        term = jnp.einsum("erd,df->ref", rowsum, columns, preferred_element_type=jnp.float32)
        total = term if total is None else total + term
    cross = lax.psum_scatter(total, "jgrp", scatter_dimension=0, tiled=True)
    factors = lax.dynamic_slice_in_dim(prefactor, jgroup * share, share, 0)
    partial_rates = jnp.einsum(
        "ref,te,re->rtf", cross, maxwell, factors, precision=lax.Precision.HIGHEST
    )
    return lax.psum_scatter(partial_rates, "energy", scatter_dimension=0, tiled=True)


def solution(mesh):
    in_specs = (
        P("jgrp", "energy", None, None),
        P("jgrp", "energy", None, None),
        P("jgrp", None),
        P("jgrp"),
        P(None, "energy"),
        P(None, "energy"),
    )
    out_specs = P(("jgrp", "energy"), None, None)
    return jax.shard_map(body, mesh=mesh, in_specs=in_specs, out_specs=out_specs, check_vma=False)
```

profile of v0, /device:TPU:2, one launch (start us, length us, event | category | flops | bytes accessed | tf_op | source)
XLA Modules:
  0.0 247.3 jit_solution(6598707829952023912)
XLA Ops:
  6.5 0.0 copy-start
  6.5 0.0 reduce-scatter.3.cloned.1.call-start
  6.6 1.3 fusion.40
  7.9 2.0 fusion.39
  9.9 5.6 %convert_bitcast_fusion.1 = bf16[16,512,256]{1,2,0:T(8,128)(2,1)} fusion(f32[]{:T(128)S(6)} %convert_element_type.61, bf16[2,16,256,256]{3,2,1,0:T(8,128)(2,1)} %param.7, bf16[2,16,256,256]{3,2,1,0:T(8,128)(2,1)} %param.6, f32[256,256]{1,0:T(8,128)S(1)} %fusion.33, s32[256]{0:T(256)S(1)} %bitcast.55), kind=kOutput, calls=%fused_computation.12 | convolution fusion | flops 1084358656 | bytes 8651780 | tf_op jit(solution)/shard_map/rc,ecd->erd/dot_general | solution.py:29
  15.5 7.9 %copy.8 = bf16[16,512,256]{2,0,1:T(8,128)(2,1)} copy(bf16[16,512,256]{1,2,0:T(8,128)(2,1)} %convert_bitcast_fusion.1) | data formatting | bytes 8388608 | tf_op jit(solution)/shard_map/convert_element_type | solution.py:31
  23.4 0.6 compare_select_fusion.3
  24.0 5.6 %convert_bitcast_fusion = bf16[16,512,256]{1,2,0:T(8,128)(2,1)} fusion(f32[]{:T(128)S(6)} %convert_element_type.68, bf16[2,16,256,256]{3,2,1,0:T(8,128)(2,1)} %param.7, bf16[2,16,256,256]{3,2,1,0:T(8,128)(2,1)} %param.6, f32[256,256]{1,0:T(8,128)S(1)} %fusion.33, s32[256]{0:T(256)S(1)} %bitcast.54), kind=kOutput, calls=%fused_computation.11 | convolution fusion | flops 1084358656 | bytes 8651780 | tf_op jit(solution)/shard_map/rc,ecd->erd/dot_general | solution.py:29
  29.6 7.9 %copy.9 = bf16[16,512,256]{2,0,1:T(8,128)(2,1)} copy(bf16[16,512,256]{1,2,0:T(8,128)(2,1)} %convert_bitcast_fusion) | data formatting | bytes 8388608 | tf_op jit(solution)/shard_map/convert_element_type | solution.py:31
  37.5 0.6 compare_select_fusion.2
  38.2 0.0 copy-start.1
  38.2 10.5 %fusion.21 = f32[512,16,512]{0,1,2:T(8,128)} fusion(bf16[16,512,256]{2,0,1:T(8,128)(2,1)} %copy.8, s32[256]{0:T(256)S(1)} %compare_select_fusion.3), kind=kOutput, calls=%fused_computation.28 | convolution fusion | flops 2147614720 | bytes 20972544 | tf_op jit(solution)/shard_map/erd,df->ref/dot_general | solution.py:32
  48.7 0.0 copy-done.1
  48.7 14.1 %add_bitcast_fusion = f32[512,16,512]{2,1,0:T(8,128)} fusion(f32[512,16,512]{0,1,2:T(8,128)} %fusion.21, bf16[16,512,256]{2,0,1:T(8,128)(2,1)S(1)} %copy-done.1, s32[256]{0:T(256)S(1)} %compare_select_fusion.2), kind=kOutput, calls=%fused_computation | convolution fusion | flops 2151809024 | bytes 37749760 | tf_op jit(solution)/shard_map/erd,df->ref/dot_general | solution.py:32
  62.7 0.0 copy-start.2
  62.7 0.0 reduce-scatter.3.cloned.1.call-update
  62.8 0.0 reduce-scatter.5.cloned.1.call-start
  62.8 0.0 copy-done
  62.8 0.1 dynamic-slice_bitcast_fusion
  62.9 0.1 copy.7
  63.0 118.3 %reduce-scatter.3.cloned.1.call-done = f32[32,16,512]{2,1,0:T(8,128)} async-done(((f32[512,16,512]{2,1,0:T(8,128)}), f32[32,16,512]{2,1,0:T(8,128)}) %reduce-scatter.3.cloned.1.call-update) | async-done | bytes 1048592 | tf_op jit(solution)/shard_map/reduce_scatter | solution.py:34
  181.3 0.0 copy-done.2
  181.3 2.7 %fusion.34 = f32[32,8,512]{2,1,0:T(8,128)} fusion(f32[32,16,512]{2,1,0:T(8,128)} %reduce-scatter.3.cloned.1.call-done, f32[16,8]{0,1:T(8,128)S(1)} %bitcast.51, f32[16,32]{0,1:T(8,128)S(1)} %copy.7), kind=kOutput, calls=%fused_computation.38 | convolution fusion | flops 25169920 | bytes 1575424 | tf_op jit(solution)/shard_map/ref,te,re->rtf/dot_general | solution.py:36
  183.9 0.0 reduce-scatter.5.cloned.1.call-update
  184.0 56.5 %reduce-scatter.5.cloned.1.call-done = f32[2,8,512]{2,1,0:T(8,128)} async-done(((f32[32,8,512]{2,1,0:T(8,128)}), f32[2,8,512]{2,1,0:T(8,128)}) %reduce-scatter.5.cloned.1.call-update) | async-done | bytes 32784 | tf_op jit(solution)/shard_map/reduce_scatter | solution.py:39
  (1 shorter events, 0.0 us)
Async XLA Ops:
  6.5 56.3 %copy-start = (f32[512,16]{0,1:T(8,128)S(1)}, f32[512,16]{0,1:T(8,128)}, u32[]{:S(2)}) copy-start(f32[512,16]{0,1:T(8,128)} %param.10) | copy-start | bytes 98308
  6.5 174.8 %reduce-scatter.3.cloned.1.call-start = ((), (), s32[]{:S(2)}) async-start(), calls=%async_computation.2 | async-start | bytes 17825792 | tf_op jit(solution)/shard_map/reduce_scatter | solution.py:34
  38.2 10.5 %copy-start.1 = (bf16[16,512,256]{2,0,1:T(8,128)(2,1)S(1)}, bf16[16,512,256]{2,0,1:T(8,128)(2,1)}, u32[]{:S(2)}) copy-start(bf16[16,512,256]{2,0,1:T(8,128)(2,1)} %copy.9) | copy-start | bytes 12582916
  62.7 118.6 %copy-start.2 = (f32[8,16]{1,0:T(8,128)S(1)}, f32[8,16]{1,0:T(8,128)}, u32[]{:S(2)}) copy-start(f32[8,16]{1,0:T(8,128)} %param.11) | copy-start | bytes 1540
  62.8 177.7 %reduce-scatter.5.cloned.1.call-start = ((), (), s32[]{:S(2)}) async-start(), calls=%async_computation.3 | async-start | bytes 557056 | tf_op jit(solution)/shard_map/reduce_scatter | solution.py:39
Sparse Core Ops, SparseCore 0:
  62.9 118.3 reduce-scatter.2
  184.1 56.3 reduce-scatter.4
where the time goes:
time: 248 us; the launch traced here: 247 us
  waiting for transfers between devices  175 us (71%)
  matrix products  38.4 us (15%)
  local copies, waits for them, and re-layouts  17.3 us (7%)
  between operations  13.5 us (5%)
  other arithmetic  3.29 us (1%)
    reduce_scatter x1, waiting for transfers between devices, body(): cross = lax.psum_scatter(total, 'jgrp', scatter_dimension=0, tiled=True)  118 us
    reduce_scatter x1, waiting for transfers between devices, body(): lax.psum_scatter(partial_rates, 'energy', scatter_dimension=0, tiled=True)  56.5 us
    dot_general x2, matrix products, body(): jnp.einsum('erd,df->ref', rowsum, columns, preferred_element_type=jnp.flo...  24.6 us
    convert_element_type x2, local copies, waits for them, and re-layouts, body(): rowsum = jnp.einsum('rc,ecd->erd', picks, weighted, preferred_element_typ...  15.8 us
    dot_general x2, matrix products, body(): jnp.einsum('rc,ecd->erd', picks, weighted, preferred_element_type=jnp.flo...  11.2 us
  transfers between devices with their start and end apart: 2, of which 2 were waited for; matrix products, arithmetic and copies ran while one was open for 0% of the time, Pallas kernels for 0%

commit v1 on v0

v1 whole, which is shorter than its diff:
```python
import functools

import jax
import jax.numpy as jnp
from jax import lax
from jax.experimental import pallas as pl
from jax.experimental.pallas import tpu as pltpu
from jax.sharding import Mesh, PartitionSpec as P

STEP = 4
GROUP = 16
HIGHEST = lax.Precision.HIGHEST


def split2(x):
    hi = x.astype(jnp.bfloat16)
    lo = (x - hi.astype(jnp.float32)).astype(jnp.bfloat16)
    return hi, lo


def iota(shape, axis):
    return lax.broadcasted_iota(jnp.int32, shape, axis)


def share_kernel(block, count_ref, level_ref, real_ref, imag_ref, pre_ref, max_ref,
                 send_ref, keep_ref, rows_ref, same_ref, scale_ref, weight_ref):
    temps, energies = max_ref.shape
    levels = pre_ref.shape[0]
    chans = real_ref.shape[-1]
    width = energies * GROUP
    step = pl.program_id(0)
    core = lax.axis_index("core")
    jgrp = lax.axis_index("y") * lax.axis_size("x") + lax.axis_index("x")
    factor = (2 * (jgrp * level_ref.shape[0] + block) + 1).astype(jnp.float32)
    eye = iota((chans, chans), 0) == iota((chans, chans), 1)

    @pl.when(step == 0)
    def _():
        lane = iota((1, chans), 1)
        seg_row = jnp.where(lane < count_ref[block], level_ref[pl.ds(block, 1), :], -1)
        seg_col = jnp.sum(
            jnp.where(eye, seg_row.astype(jnp.float32), 0.0), axis=1, keepdims=True
        ).astype(jnp.int32)
        same = (seg_col == seg_row) & (seg_col >= 0)
        earlier = same & (iota((chans, chans), 1) < iota((chans, chans), 0))
        taken = jnp.max(jnp.where(earlier, 1.0, 0.0), axis=1, keepdims=True)
        same_ref[...] = jnp.where(same & (taken == 0.0), 1.0, 0.0).astype(jnp.bfloat16)
        picks = jnp.where(seg_col == iota((chans, levels), 1), 1.0, 0.0)
        spread = jnp.where(iota((energies, width), 1) // GROUP == iota((energies, width), 0), 1.0, 0.0)
        own = jnp.dot(picks, pre_ref[...], precision=HIGHEST, preferred_element_type=jnp.float32)
        scale_ref[...] = jnp.dot(own, spread, precision=HIGHEST, preferred_element_type=jnp.float32)
        wide = jnp.dot(max_ref[...], spread, precision=HIGHEST, preferred_element_type=jnp.float32)
        hit = iota((GROUP, width), 1) % GROUP == iota((GROUP, width), 0)
        for t in range(temps):
            weight_ref[t * GROUP:(t + 1) * GROUP, :] = jnp.where(hit, wide[t:t + 1, :], 0.0)

    delta = jnp.where(eye, 1.0, 0.0)
    for e in range(STEP):
        real = real_ref[0, e].astype(jnp.float32)
        imag = imag_ref[0, e].astype(jnp.float32)
        weighted = (((delta - real) ** 2 + imag ** 2) * factor).astype(jnp.bfloat16)
        rowsum = jnp.dot(same_ref[...], weighted, preferred_element_type=jnp.float32)
        rows_ref[step * STEP + e] = rowsum.astype(jnp.bfloat16)

    @pl.when(step == pl.num_programs(0) - 1)
    def _():
        half = chans // 2
        for out_ref, base in ((send_ref, (1 - core) * half), (keep_ref, core * half)):
            for group in range(half // GROUP):
                at = pl.ds(pl.multiple_of(base + group * GROUP, GROUP), GROUP)
                part = rows_ref[:, at, :].reshape(width, chans)
                own = scale_ref[at, :]
                mix = weight_ref[...] * jnp.concatenate([own] * temps, axis=0)
                hi, lo = split2(mix)
                both = jnp.dot(jnp.concatenate([hi, lo], axis=0), part,
                               preferred_element_type=jnp.float32)
                total = both[:temps * GROUP] + both[temps * GROUP:]
                out_ref[:, group * GROUP:(group + 1) * GROUP, :] = total.reshape(temps, GROUP, chans)


def share(block, counts, level_map, s_real, s_imag, prefactor, maxwell):
    energies, chans = s_real.shape[1], s_real.shape[2]
    temps, levels = maxwell.shape[0], prefactor.shape[0]
    width = energies * GROUP
    out = jax.ShapeDtypeStruct((temps, chans // 2, chans), jnp.float32)
    whole = pl.BlockSpec(memory_space=pltpu.VMEM)
    parts = pl.BlockSpec((1, STEP, chans, chans), lambda e: (block, e, 0, 0))
    return pl.pallas_call(
        functools.partial(share_kernel, block),
        grid=(energies // STEP,),
        out_shape=[out, out],
        in_specs=[pl.BlockSpec(memory_space=pltpu.SMEM), whole, parts, parts, whole, whole],
        out_specs=[pl.BlockSpec((temps, chans // 2, chans), lambda e: (0, 0, 0))] * 2,
        scratch_shapes=[
            pltpu.VMEM((energies, chans, chans), jnp.bfloat16),
            pltpu.VMEM((chans, chans), jnp.bfloat16),
            pltpu.VMEM((chans, width), jnp.float32),
            pltpu.VMEM((temps * GROUP, width), jnp.float32),
        ],
        compiler_params=pltpu.CompilerParams(vmem_limit_bytes=40 * 2**20),
        cost_estimate=pl.CostEstimate(flops=2 * 2 * energies * chans**3, transcendentals=0,
                                      bytes_accessed=4 * energies * chans**2 + 8 * temps * chans**2),
        name="share",
    )(counts, level_map, s_real, s_imag, prefactor, maxwell)


def spread_kernel(count_ref, level_ref, mine_ref, other_ref, out_ref):
    blocks, half, chans = mine_ref.shape
    rows, levels = out_ref.shape
    core = lax.axis_index("core")
    lane = iota((1, chans), 1)
    row = iota((rows, chans), 0)
    wanted = row // 2 * 4 + core * 2 + row % 2
    for block in range(blocks):
        seg = jnp.where(lane < count_ref[block], level_ref[pl.ds(block, 1), :], -1)
        columns = jnp.where(iota((levels, chans), 0) == seg, 1.0, 0.0).astype(jnp.bfloat16)
        picks = jnp.where(wanted == seg, 1.0, 0.0).astype(jnp.bfloat16)
        mine, other = mine_ref[block], other_ref[block]
        first = jnp.where(core == 0, mine, other)
        second = jnp.where(core == 0, other, mine)
        both = jnp.concatenate([first, second], axis=0)
        hi, lo = split2(both)
        turn = (((1,), (1,)), ((), ()))
        wide = lax.dot_general(hi, columns, turn, preferred_element_type=jnp.float32)
        wide += lax.dot_general(lo, columns, turn, preferred_element_type=jnp.float32)
        hi, lo = split2(wide)
        term = jnp.dot(picks, hi, preferred_element_type=jnp.float32)
        term += jnp.dot(picks, lo, preferred_element_type=jnp.float32)
        if block == 0:
            out_ref[...] = term
        else:
            out_ref[...] += term


def spread(counts, level_map, mine, other, levels):
    whole = pl.BlockSpec(memory_space=pltpu.VMEM)
    return pl.pallas_call(
        spread_kernel,
        out_shape=jax.ShapeDtypeStruct((levels // 2, levels), jnp.float32),
        in_specs=[pl.BlockSpec(memory_space=pltpu.SMEM), whole, whole, whole],
        out_specs=whole,
        compiler_params=pltpu.CompilerParams(vmem_limit_bytes=40 * 2**20),
        name="spread",
    )(counts, level_map, mine, other)


def ring_sum(z, n, keep, other):
    rows = keep.shape[1]
    half = rows // 2

    def own(t, low, high):
        def cut(x):
            return lax.dynamic_slice_in_dim(x, lax.rem(t + n, n), 1, 0)[0, low:high]
        return cut(keep) + cut(other)

    up = [(i, (i + 1) % n) for i in range(n)]
    down = [(i, (i - 1) % n) for i in range(n)]
    reach = n // 2
    forward = lax.ppermute(own(z + reach, 0, half), "z", up)
    backward = lax.ppermute(own(z - reach, half, rows), "z", down)
    forward = jnp.concatenate([forward + own(z + reach - 1, 0, half), own(z + reach - 1, half, rows)])
    backward = jnp.concatenate([own(z - reach + 1, 0, half), backward + own(z - reach + 1, half, rows)])
    for left in range(reach - 1, 0, -1):
        forward = lax.ppermute(forward, "z", up)
        backward = lax.ppermute(backward, "z", down)
        if left > 1:
            forward = forward + own(z + left - 1, 0, rows)
            backward = backward + own(z - left + 1, 0, rows)
    return forward + backward + own(z, 0, rows)


def body(s_real, s_imag, level_map, channel_count, prefactor, maxwell):
    blocks = s_real.shape[0]
    levels = prefactor.shape[0]
    temps = maxwell.shape[0]
    n = lax.axis_size("z")
    z = lax.axis_index("z")
    swap = [(0, 1), (1, 0)]
    sums = []
    for block in range(blocks):
        send, keep = share(block, channel_count, level_map, s_real, s_imag, prefactor, maxwell)
        other = lax.ppermute(send, "core", swap)
        sums.append(ring_sum(z, n, keep, other))
    mine = jnp.stack(sums)
    other = lax.ppermute(mine, "core", swap)
    part = spread(channel_count, level_map, mine, other, levels)
    groups = lax.axis_size("y") * lax.axis_size("x")
    part = part.reshape(groups, levels // 2 // groups, levels)
    part = lax.all_to_all(part, ("y", "x"), 0, 0, tiled=True).sum(0)
    part = lax.all_to_all(part.reshape(n, part.shape[0] // n, levels), "z", 0, 0, tiled=True)
    return jnp.transpose(part, (1, 0, 2))


def solution(mesh):
    fine = Mesh(mesh.devices.reshape(4, 4, 8, 2), ("y", "x", "z", "core"))
    jgrp, energy = ("y", "x"), ("z", "core")
    in_specs = (
        P(jgrp, energy, None, None),
        P(jgrp, energy, None, None),
        P(jgrp, None),
        P(jgrp),
        P(None, energy),
        P(None, energy),
    )
    out_specs = P(("y", "x", "z", "core"), None, None)
    return jax.shard_map(body, mesh=fine, in_specs=in_specs, out_specs=out_specs, check_vma=False)
```

time: 248 us -> 97.5 us (0.39)
  waiting for transfers between devices: 175 us -> 11.1 us
  matrix products: 38.4 us -> 0 us
  blocking collectives: 0 us -> 30.1 us
  starting transfers between devices: 0.04 us -> 25.4 us
  between operations: 13.5 us -> 0.17 us
  Pallas kernels: 0 us -> 12.2 us
  local copies, waits for them, and re-layouts: 17.3 us -> 7.93 us
  other arithmetic: 3.29 us -> 9.86 us
    reduce_scatter x2 -> x0, waiting for transfers between devices: 175 us -> none  [the longest x1 118 us: body(): cross = lax.psum_scatter(total, 'jgrp', scatter_dimension=0, tiled=True)]
    dot_general x5 -> x0, matrix products: 38.4 us -> none  [the longest x2 24.6 us: body(): jnp.einsum('erd,df->ref', rowsum, columns, preferred_element_type=jnp.flo...]
    all_to_all x0 -> x2, blocking collectives: none -> 30.1 us  [the longest x1 17.7 us: body(): part = lax.all_to_all(part, ('y', 'x'), 0, 0, tiled=True).sum(0)]
    ppermute x0 -> x19, starting transfers between devices: none -> 25.4 us  [the longest x6 13.9 us: ring_sum(): backward = lax.ppermute(backward, 'z', down)]
    convert_element_type x2 -> x0, local copies, waits for them, and re-layouts: 15.8 us -> none  [body(): rowsum = jnp.einsum('rc,ecd->erd', picks, weighted, preferred_element_typ...]
    pallas_call x0 -> x3, Pallas kernels: none -> 12.2 us  [the longest x2 10.6 us: share(): pl.pallas_call(functools.partial(share_kernel, block), grid=(energies //...]
    ppermute x0 -> x19, waiting for transfers between devices: none -> 11.1 us  [the longest x6 7.31 us: ring_sum(): forward = lax.ppermute(forward, 'z', up)]
    add x0 -> x8, other arithmetic: none -> 7.88 us  [the longest x4 4.13 us: ring_sum(): backward = backward + own(z - left + 1, 0, rows)]
  transfers between devices with their start and end apart: 2 -> 19, of which waited for: 2 -> 7; matrix products, arithmetic and copies ran while one was open for 0% -> 9% of each run, Pallas kernels for 0% -> 5%
where the time goes in v1:
time: 97.5 us; the launch traced here: 96.8 us
  blocking collectives  30.1 us (31%)
  starting transfers between devices  25.4 us (26%)
  Pallas kernels  12.2 us (13%)
  waiting for transfers between devices  11.1 us (11%)
  other arithmetic  9.86 us (10%)
  local copies, waits for them, and re-layouts  7.93 us (8%)
    all_to_all x1, blocking collectives, body(): part = lax.all_to_all(part, ('y', 'x'), 0, 0, tiled=True).sum(0)  17.7 us
    ppermute x6, starting transfers between devices, ring_sum(): backward = lax.ppermute(backward, 'z', down)  13.9 us
    all_to_all x1, blocking collectives, body(): lax.all_to_all(part.reshape(n, part.shape[0] // n, levels), 'z', 0, 0, ti...  12.3 us
    pallas_call x2, Pallas kernels, share(): pl.pallas_call(functools.partial(share_kernel, block), grid=(energies //...  10.6 us
    ppermute x2, starting transfers between devices, ring_sum(): backward = lax.ppermute(own(z - reach, half, rows), 'z', down)  9.24 us
    ppermute x6, waiting for transfers between devices, ring_sum(): forward = lax.ppermute(forward, 'z', up)  7.31 us
    unnamed x15, local copies, waits for them, and re-layouts  7.29 us
    add x4, other arithmetic, ring_sum(): backward = backward + own(z - left + 1, 0, rows)  4.13 us
  transfers between devices with their start and end apart: 19, of which 7 were waited for; matrix products, arithmetic and copies ran while one was open for 9% of the time, Pallas kernels for 5%

profile of v1, /device:TPU:2, one launch (start us, length us, event | category | flops | bytes accessed | tf_op | source)
XLA Modules:
  0.0 96.8 jit_solution(278006262105190654)
XLA Ops:
  0.9 2.2 %copy-done = bf16[2,16,256,256]{3,2,1,0:T(8,128)(2,1)S(1)} copy-done((bf16[2,16,256,256]{3,2,1,0:T(8,128)(2,1)S(1)}, bf16[2,16,256,256]{3,2,1,0:T(8,128)(2,1)}, u32[]{:S(2)}) %copy-start) | copy-done | bytes 4194328
  3.1 2.2 %copy-done.1 = bf16[2,16,256,256]{3,2,1,0:T(8,128)(2,1)S(1)} copy-done((bf16[2,16,256,256]{3,2,1,0:T(8,128)(2,1)S(1)}, bf16[2,16,256,256]{3,2,1,0:T(8,128)(2,1)}, u32[]{:S(2)}) %copy-start.1) | copy-done | bytes 4194328
  7.3 5.8 %share.3 = (f32[8,128,256]{2,1,0:T(8,128)}, f32[8,128,256]{2,1,0:T(8,128)S(1)}) custom-call(s32[2]{0:T(128)S(1)} %copy-done.5, s32[2,256]{1,0:T(2,128)S(1)} %copy-done.2, bf16[2,16,256,256]{3,2,1,0:T(8,128)(2,1)S(1)} %copy-done, bf16[2,16,256,256]{3,2,1,0:T(8,128)(2,1)S(1)} %copy-done.1, f32[512,16]{1,0:T(8,128)S(1)} %copy.9.pre_ref, f32[8,16]{1,0:T(8,128)S(1)} %copy-done.4), custom_call_target="tpu_custom_call" | custom-call | flops 1073741824 | bytes 8388608 | tf_op jit(solution)/shard_map/share/pallas_call | solution.py:88
  13.1 4.8 %share.2 = (f32[8,128,256]{2,1,0:T(8,128)S(1)}, f32[8,128,256]{2,1,0:T(8,128)S(1)}) custom-call(s32[2]{0:T(128)S(1)} %copy-done.5, s32[2,256]{1,0:T(2,128)S(1)} %copy-done.2, bf16[2,16,256,256]{3,2,1,0:T(8,128)(2,1)S(1)} %copy-done, bf16[2,16,256,256]{3,2,1,0:T(8,128)(2,1)S(1)} %copy-done.1, f32[512,16]{1,0:T(8,128)S(1)} %copy.9.pre_ref, f32[8,16]{1,0:T(8,128)S(1)} %copy-done.4), custom_call_target="tpu_custom_call" | custom-call | flops 1073741824 | bytes 8388608 | tf_op jit(solution)/shard_map/share/pallas_call | solution.py:88
  18.5 1.0 %fusion.5 = (f32[64,256]{1,0:T(8,128)S(1)}, f32[64,256]{1,0:T(8,128)S(1)}, f32[64,256]{1,0:T(8,128)S(1)}, f32[64,256]{1,0:T(8,128)S(1)}) fusion(f32[8,128,256]{2,1,0:T(8,128)} %collective-permute-done.9, s32[]{:T(128)S(6)} %select_n.22, f32[8,128,256]{2,1,0:T(8,128)S(1)} %get-tuple-element.11, s32[]{:T(128)S(6)} %select_n.23, s32[]{:T(128)S(6)} %add.434, ...), kind=kLoop, calls=%fused_computation.23 | loop fusion | flops 65536 | bytes 786452 | tf_op jit(solution)/shard_map/add | solution.py:154
  19.5 5.9 %collective-permute-start.14 = (f32[64,256]{1,0:T(8,128)S(1)}, f32[64,256]{1,0:T(8,128)S(1)}, u32[]{:S(2)}, u32[]{:S(2)}) collective-permute-start(f32[64,256]{1,0:T(8,128)S(1)} %get-tuple-element.28), channel_id=1, source_target_pairs={{0,14},{2,0},{4,2},{6,4},{8,6},{10,8},{12,10},{14,12},{1,15},{3,1}... | collective-permute-start | bytes 196616 | tf_op jit(solution)/shard_map/ppermute | solution.py:160
  25.4 1.0 %fusion.13 = (f32[64,256]{1,0:T(8,128)S(1)}, f32[64,256]{1,0:T(8,128)S(1)}, f32[64,256]{1,0:T(8,128)S(1)}, f32[64,256]{1,0:T(8,128)S(1)}) fusion(f32[8,128,256]{2,1,0:T(8,128)} %collective-permute-done, s32[]{:T(128)S(6)} %select_n.22, f32[8,128,256]{2,1,0:T(8,128)S(1)} %get-tuple-element.9, s32[]{:T(128)S(6)} %select_n.23, s32[]{:T(128)S(6)} %add.434, ...), kind=kLoop, calls=%fused_computation.37 | loop fusion | flops 65536 | bytes 786452 | tf_op jit(solution)/shard_map/add | solution.py:154
  26.4 3.3 %collective-permute-start.5 = (f32[64,256]{1,0:T(8,128)S(1)}, f32[64,256]{1,0:T(8,128)S(1)}, u32[]{:S(2)}, u32[]{:S(2)}) collective-permute-start(f32[64,256]{1,0:T(8,128)S(1)} %get-tuple-element.18), channel_id=1, source_target_pairs={{0,14},{2,0},{4,2},{6,4},{8,6},{10,8},{12,10},{14,12},{1,15},{3,1}... | collective-permute-start | bytes 196616 | tf_op jit(solution)/shard_map/ppermute | solution.py:160
  29.8 1.2 %collective-permute-done.10 = f32[64,256]{1,0:T(8,128)S(1)} collective-permute-done((f32[64,256]{1,0:T(8,128)S(1)}, f32[64,256]{1,0:T(8,128)S(1)}, u32[]{:S(2)}, u32[]{:S(2)}) %collective-permute-start.10) | collective-permute-done | bytes 65568 | tf_op jit(solution)/shard_map/ppermute | solution.py:159
  30.9 0.9 fusion.3
  31.8 2.2 %collective-permute-start.15 = (f32[128,256]{1,0:T(8,128)S(1)}, f32[128,256]{1,0:T(8,128)S(1)}, u32[]{:S(2)}, u32[]{:S(2)}) collective-permute-start(f32[128,256]{1,0:T(8,128)S(1)} %pad_maximum_fusion.4), channel_id=1, source_target_pairs={{0,14},{2,0},{4,2},{6,4},{8,6},{10,8},{12,10},{14,12},{1,15},{3,1}... | collective-permute-start | bytes 393224 | tf_op jit(solution)/shard_map/ppermute | solution.py:165
  34.1 1.1 %collective-permute-done.1 = f32[64,256]{1,0:T(8,128)S(1)} collective-permute-done((f32[64,256]{1,0:T(8,128)S(1)}, f32[64,256]{1,0:T(8,128)S(1)}, u32[]{:S(2)}, u32[]{:S(2)}) %collective-permute-start.1) | collective-permute-done | bytes 65568 | tf_op jit(solution)/shard_map/ppermute | solution.py:159
  35.2 0.9 fusion.11
  36.2 2.2 %collective-permute-start.6 = (f32[128,256]{1,0:T(8,128)S(1)}, f32[128,256]{1,0:T(8,128)S(1)}, u32[]{:S(2)}, u32[]{:S(2)}) collective-permute-start(f32[128,256]{1,0:T(8,128)S(1)} %pad_maximum_fusion.2), channel_id=1, source_target_pairs={{0,14},{2,0},{4,2},{6,4},{8,6},{10,8},{12,10},{14,12},{1,15},{3,1}... | collective-permute-start | bytes 393224 | tf_op jit(solution)/shard_map/ppermute | solution.py:165
  38.4 1.8 %collective-permute-done.11 = f32[128,256]{1,0:T(8,128)S(1)} collective-permute-done((f32[128,256]{1,0:T(8,128)S(1)}, f32[128,256]{1,0:T(8,128)S(1)}, u32[]{:S(2)}, u32[]{:S(2)}) %collective-permute-start.11) | collective-permute-done | bytes 131104 | tf_op jit(solution)/shard_map/ppermute | solution.py:164
  40.3 1.0 %bitcast_add_fusion.2 = (f32[128,256]{1,0:T(8,128)S(1)}, f32[128,256]{1,0:T(8,128)S(1)}) fusion(f32[128,256]{1,0:T(8,128)S(1)} %collective-permute-done.15, f32[8,128,256]{2,1,0:T(8,128)} %collective-permute-done.9, s32[]{:T(128)S(6)} %select_n.24, f32[8,128,256]{2,1,0:T(8,128)S(1)} %get-tuple-element.11, f32[128,256]{1,0:T(8,128)S(1)} %collective-permute-done.11, ...), kind=kLoop, calls=%fused_computation.8 | loop fusion | flops 131072 | bytes 1048584 | tf_op jit(solution)/shard_map/add | solution.py:168
  41.3 1.7 %collective-permute-start.16 = (f32[128,256]{1,0:T(8,128)S(1)}, f32[128,256]{1,0:T(8,128)S(1)}, u32[]{:S(2)}, u32[]{:S(2)}) collective-permute-start(f32[128,256]{1,0:T(8,128)S(1)} %get-tuple-element.25), channel_id=1, source_target_pairs={{0,14},{2,0},{4,2},{6,4},{8,6},{10,8},{12,10},{14,12},{1,15},{3,1}... | collective-permute-start | bytes 393224 | tf_op jit(solution)/shard_map/ppermute | solution.py:165
  43.6 1.3 %collective-permute-done.2 = f32[128,256]{1,0:T(8,128)S(1)} collective-permute-done((f32[128,256]{1,0:T(8,128)S(1)}, f32[128,256]{1,0:T(8,128)S(1)}, u32[]{:S(2)}, u32[]{:S(2)}) %collective-permute-start.2) | collective-permute-done | bytes 131104 | tf_op jit(solution)/shard_map/ppermute | solution.py:164
  44.8 1.0 %bitcast_add_fusion.7 = (f32[128,256]{1,0:T(8,128)S(1)}, f32[128,256]{1,0:T(8,128)S(1)}) fusion(f32[128,256]{1,0:T(8,128)S(1)} %collective-permute-done.6, f32[8,128,256]{2,1,0:T(8,128)} %collective-permute-done, s32[]{:T(128)S(6)} %select_n.24, f32[8,128,256]{2,1,0:T(8,128)S(1)} %get-tuple-element.9, f32[128,256]{1,0:T(8,128)S(1)} %collective-permute-done.2, ...), kind=kLoop, calls=%fused_computation.14 | loop fusion | flops 131072 | bytes 1048584 | tf_op jit(solution)/shard_map/add | solution.py:168
  45.9 1.4 %collective-permute-start.7 = (f32[128,256]{1,0:T(8,128)S(1)}, f32[128,256]{1,0:T(8,128)S(1)}, u32[]{:S(2)}, u32[]{:S(2)}) collective-permute-start(f32[128,256]{1,0:T(8,128)S(1)} %get-tuple-element.15), channel_id=1, source_target_pairs={{0,14},{2,0},{4,2},{6,4},{8,6},{10,8},{12,10},{14,12},{1,15},{3,1}... | collective-permute-start | bytes 393224 | tf_op jit(solution)/shard_map/ppermute | solution.py:165
  48.0 2.2 %collective-permute-done.12 = f32[128,256]{1,0:T(8,128)S(1)} collective-permute-done((f32[128,256]{1,0:T(8,128)S(1)}, f32[128,256]{1,0:T(8,128)S(1)}, u32[]{:S(2)}, u32[]{:S(2)}) %collective-permute-start.12) | collective-permute-done | bytes 131104 | tf_op jit(solution)/shard_map/ppermute | solution.py:164
  50.2 1.0 %bitcast_add_fusion.1 = (f32[128,256]{1,0:T(8,128)S(1)}, f32[128,256]{1,0:T(8,128)S(1)}) fusion(f32[128,256]{1,0:T(8,128)S(1)} %collective-permute-done.16, f32[8,128,256]{2,1,0:T(8,128)} %collective-permute-done.9, s32[]{:T(128)S(6)} %select_n.25, f32[8,128,256]{2,1,0:T(8,128)S(1)} %get-tuple-element.11, f32[128,256]{1,0:T(8,128)S(1)} %collective-permute-done.12, ...), kind=kLoop, calls=%fused_computation.7 | loop fusion | flops 131072 | bytes 1048584 | tf_op jit(solution)/shard_map/add | solution.py:168
  51.3 3.2 %collective-permute-start.17 = (f32[128,256]{1,0:T(8,128)S(1)}, f32[128,256]{1,0:T(8,128)S(1)}, u32[]{:S(2)}, u32[]{:S(2)}) collective-permute-start(f32[128,256]{1,0:T(8,128)S(1)} %get-tuple-element.23), channel_id=1, source_target_pairs={{0,14},{2,0},{4,2},{6,4},{8,6},{10,8},{12,10},{14,12},{1,15},{3,1}... | collective-permute-start | bytes 393224 | tf_op jit(solution)/shard_map/ppermute | solution.py:165
  54.6 1.0 %bitcast_add_fusion.6 = (f32[128,256]{1,0:T(8,128)S(1)}, f32[128,256]{1,0:T(8,128)S(1)}) fusion(f32[128,256]{1,0:T(8,128)S(1)} %collective-permute-done.7, f32[8,128,256]{2,1,0:T(8,128)} %collective-permute-done, s32[]{:T(128)S(6)} %select_n.25, f32[8,128,256]{2,1,0:T(8,128)S(1)} %get-tuple-element.9, f32[128,256]{1,0:T(8,128)S(1)} %collective-permute-done.3, ...), kind=kLoop, calls=%fused_computation.13 | loop fusion | flops 131072 | bytes 1048584 | tf_op jit(solution)/shard_map/add | solution.py:168
  55.7 3.2 %collective-permute-start.8 = (f32[128,256]{1,0:T(8,128)S(1)}, f32[128,256]{1,0:T(8,128)S(1)}, u32[]{:S(2)}, u32[]{:S(2)}) collective-permute-start(f32[128,256]{1,0:T(8,128)S(1)} %get-tuple-element.13), channel_id=1, source_target_pairs={{0,14},{2,0},{4,2},{6,4},{8,6},{10,8},{12,10},{14,12},{1,15},{3,1}... | collective-permute-start | bytes 393224 | tf_op jit(solution)/shard_map/ppermute | solution.py:165
  58.9 0.9 fusion
  59.9 2.0 %collective-permute-done.4 = f32[128,256]{1,0:T(8,128)S(1)} collective-permute-done((f32[128,256]{1,0:T(8,128)S(1)}, f32[128,256]{1,0:T(8,128)S(1)}, u32[]{:S(2)}, u32[]{:S(2)}) %collective-permute-start.4) | collective-permute-done | bytes 131104 | tf_op jit(solution)/shard_map/ppermute | solution.py:164
  61.9 0.9 fusion.1
  62.9 1.5 %collective-permute-done.18.other_ref = f32[2,128,256]{2,1,0:T(8,128)S(1)} collective-permute-done((f32[2,128,256]{2,1,0:T(8,128)S(1)}, f32[2,128,256]{2,1,0:T(8,128)S(1)}, u32[]{:S(2)}, u32[]{:S(2)}) %collective-permute-start.18) | collective-permute-done | bytes 262176 | tf_op jit(solution)/shard_map/ppermute | solution.py:185
  64.5 1.6 %spread.1 = f32[256,512]{1,0:T(8,128)S(1)} custom-call(s32[2]{0:T(128)S(1)} %copy-done.6, s32[2,256]{1,0:T(2,128)S(1)} %copy-done.3, f32[2,128,256]{2,1,0:T(8,128)S(1)} %pad_maximum_fusion.mine_ref, f32[2,128,256]{2,1,0:T(8,128)S(1)} %collective-permute-done.18.other_ref), custom_call_target="tpu_custom_call" | custom-call | tf_op jit(solution)/shard_map/spread/pallas_call | solution.py:137
  66.1 17.7 %all_to_all.10 = f32[16,16,512]{2,1,0:T(8,128)S(1)} all-to-all(f32[16,16,512]{2,1,0:T(8,128)S(1)} %bitcast.62), channel_id=1, replica_groups=mesh['y'=4,'x'=4,'z'=8,'core'=2] {'y','x'}, dimensions={0} | all-to-all | bytes 1048576 | tf_op jit(solution)/shard_map/all_to_all | solution.py:189
  83.9 12.3 %all_to_all.11 = f32[8,2,512]{2,1,0:T(2,128)S(1)} all-to-all(f32[8,2,512]{2,1,0:T(2,128)S(1)} %reshape.29), channel_id=1, replica_groups=mesh['y'=4,'x'=4,'z'=8,'core'=2] {'z'}, dimensions={0} | all-to-all | bytes 65536 | tf_op jit(solution)/shard_map/all_to_all | solution.py:190
  (44 shorter events, 6.0 us)
Async XLA Ops:
  0.9 2.2 %copy-start = (bf16[2,16,256,256]{3,2,1,0:T(8,128)(2,1)S(1)}, bf16[2,16,256,256]{3,2,1,0:T(8,128)(2,1)}, u32[]{:S(2)}) copy-start(bf16[2,16,256,256]{3,2,1,0:T(8,128)(2,1)} %real_ref.3) | copy-start | bytes 12582916
  3.1 2.2 %copy-start.1 = (bf16[2,16,256,256]{3,2,1,0:T(8,128)(2,1)S(1)}, bf16[2,16,256,256]{3,2,1,0:T(8,128)(2,1)}, u32[]{:S(2)}) copy-start(bf16[2,16,256,256]{3,2,1,0:T(8,128)(2,1)} %imag_ref.3) | copy-start | bytes 12582916
  5.3 0.7 copy-start.2
  6.0 0.7 copy-start.4
  6.6 0.7 copy-start.5
  13.1 5.4 %collective-permute-start.9 = (f32[8,128,256]{2,1,0:T(8,128)}, f32[8,128,256]{2,1,0:T(8,128)}, u32[]{:S(2)}, u32[]{:S(2)}) collective-permute-start(f32[8,128,256]{2,1,0:T(8,128)} %get-tuple-element.12), channel_id=1, source_target_pairs={{0,1},{1,0},{2,3},{3,2},{4,5},{5,4},{6,7},{7,6},{8,9},{9,8},{10,11... | collective-permute-start | bytes 3145736 | tf_op jit(solution)/shard_map/ppermute | solution.py:182
  17.9 7.5 %collective-permute-start = (f32[8,128,256]{2,1,0:T(8,128)S(1)}, f32[8,128,256]{2,1,0:T(8,128)}, u32[]{:S(2)}, u32[]{:S(2)}) collective-permute-start(f32[8,128,256]{2,1,0:T(8,128)S(1)} %get-tuple-element.10), channel_id=1, source_target_pairs={{0,1},{1,0},{2,3},{3,2},{4,5},{5,4},{6,7},{7,6},{8,9},{9,8},{10,11... | collective-permute-start | bytes 3145736 | tf_op jit(solution)/shard_map/ppermute | solution.py:182
  19.5 10.2 %collective-permute-start.14 = (f32[64,256]{1,0:T(8,128)S(1)}, f32[64,256]{1,0:T(8,128)S(1)}, u32[]{:S(2)}, u32[]{:S(2)}) collective-permute-start(f32[64,256]{1,0:T(8,128)S(1)} %get-tuple-element.28), channel_id=1, source_target_pairs={{0,14},{2,0},{4,2},{6,4},{8,6},{10,8},{12,10},{14,12},{1,15},{3,1}... | collective-permute-start | bytes 196616 | tf_op jit(solution)/shard_map/ppermute | solution.py:160
  25.4 5.5 %collective-permute-start.10 = (f32[64,256]{1,0:T(8,128)S(1)}, f32[64,256]{1,0:T(8,128)S(1)}, u32[]{:S(2)}, u32[]{:S(2)}) collective-permute-start(f32[64,256]{1,0:T(8,128)S(1)} %get-tuple-element.30), channel_id=1, source_target_pairs={{0,2},{2,4},{4,6},{6,8},{8,10},{10,12},{12,14},{14,0},{1,3},{3,5},... | collective-permute-start | bytes 196616 | tf_op jit(solution)/shard_map/ppermute | solution.py:159
  26.4 38.1 %copy-start.3 = (s32[2,256]{1,0:T(2,128)S(1)}, s32[2,256]{1,0:T(2,128)}, u32[]{:S(2)}) copy-start(s32[2,256]{1,0:T(2,128)} %level_ref.5) | copy-start | bytes 6148
  26.4 38.0 %copy-start.6 = (s32[2]{0:T(128)S(1)}, s32[2]{0:T(128)}, u32[]{:S(2)}) copy-start(s32[2]{0:T(128)} %count_ref.5) | copy-start | bytes 28
  26.4 7.7 %collective-permute-start.5 = (f32[64,256]{1,0:T(8,128)S(1)}, f32[64,256]{1,0:T(8,128)S(1)}, u32[]{:S(2)}, u32[]{:S(2)}) collective-permute-start(f32[64,256]{1,0:T(8,128)S(1)} %get-tuple-element.18), channel_id=1, source_target_pairs={{0,14},{2,0},{4,2},{6,4},{8,6},{10,8},{12,10},{14,12},{1,15},{3,1}... | collective-permute-start | bytes 196616 | tf_op jit(solution)/shard_map/ppermute | solution.py:160
  29.8 5.5 %collective-permute-start.1 = (f32[64,256]{1,0:T(8,128)S(1)}, f32[64,256]{1,0:T(8,128)S(1)}, u32[]{:S(2)}, u32[]{:S(2)}) collective-permute-start(f32[64,256]{1,0:T(8,128)S(1)} %get-tuple-element.20), channel_id=1, source_target_pairs={{0,2},{2,4},{4,6},{6,8},{8,10},{10,12},{12,14},{14,0},{1,3},{3,5},... | collective-permute-start | bytes 196616 | tf_op jit(solution)/shard_map/ppermute | solution.py:159
  31.8 6.6 %collective-permute-start.15 = (f32[128,256]{1,0:T(8,128)S(1)}, f32[128,256]{1,0:T(8,128)S(1)}, u32[]{:S(2)}, u32[]{:S(2)}) collective-permute-start(f32[128,256]{1,0:T(8,128)S(1)} %pad_maximum_fusion.4), channel_id=1, source_target_pairs={{0,14},{2,0},{4,2},{6,4},{8,6},{10,8},{12,10},{14,12},{1,15},{3,1}... | collective-permute-start | bytes 393224 | tf_op jit(solution)/shard_map/ppermute | solution.py:165
  34.0 6.3 %collective-permute-start.11 = (f32[128,256]{1,0:T(8,128)S(1)}, f32[128,256]{1,0:T(8,128)S(1)}, u32[]{:S(2)}, u32[]{:S(2)}) collective-permute-start(f32[128,256]{1,0:T(8,128)S(1)} %pad_maximum_fusion.3), channel_id=1, source_target_pairs={{0,2},{2,4},{4,6},{6,8},{8,10},{10,12},{12,14},{14,0},{1,3},{3,5},... | collective-permute-start | bytes 393224 | tf_op jit(solution)/shard_map/ppermute | solution.py:164
  36.2 7.4 %collective-permute-start.6 = (f32[128,256]{1,0:T(8,128)S(1)}, f32[128,256]{1,0:T(8,128)S(1)}, u32[]{:S(2)}, u32[]{:S(2)}) collective-permute-start(f32[128,256]{1,0:T(8,128)S(1)} %pad_maximum_fusion.2), channel_id=1, source_target_pairs={{0,14},{2,0},{4,2},{6,4},{8,6},{10,8},{12,10},{14,12},{1,15},{3,1}... | collective-permute-start | bytes 393224 | tf_op jit(solution)/shard_map/ppermute | solution.py:165
  38.3 6.5 %collective-permute-start.2 = (f32[128,256]{1,0:T(8,128)S(1)}, f32[128,256]{1,0:T(8,128)S(1)}, u32[]{:S(2)}, u32[]{:S(2)}) collective-permute-start(f32[128,256]{1,0:T(8,128)S(1)} %pad_maximum_fusion.1), channel_id=1, source_target_pairs={{0,2},{2,4},{4,6},{6,8},{8,10},{10,12},{12,14},{14,0},{1,3},{3,5},... | collective-permute-start | bytes 393224 | tf_op jit(solution)/shard_map/ppermute | solution.py:164
  41.3 6.7 %collective-permute-start.16 = (f32[128,256]{1,0:T(8,128)S(1)}, f32[128,256]{1,0:T(8,128)S(1)}, u32[]{:S(2)}, u32[]{:S(2)}) collective-permute-start(f32[128,256]{1,0:T(8,128)S(1)} %get-tuple-element.25), channel_id=1, source_target_pairs={{0,14},{2,0},{4,2},{6,4},{8,6},{10,8},{12,10},{14,12},{1,15},{3,1}... | collective-permute-start | bytes 393224 | tf_op jit(solution)/shard_map/ppermute | solution.py:165
  43.0 7.3 %collective-permute-start.12 = (f32[128,256]{1,0:T(8,128)S(1)}, f32[128,256]{1,0:T(8,128)S(1)}, u32[]{:S(2)}, u32[]{:S(2)}) collective-permute-start(f32[128,256]{1,0:T(8,128)S(1)} %get-tuple-element.26), channel_id=1, source_target_pairs={{0,2},{2,4},{4,6},{6,8},{8,10},{10,12},{12,14},{14,0},{1,3},{3,5},... | collective-permute-start | bytes 393224 | tf_op jit(solution)/shard_map/ppermute | solution.py:164
  45.9 8.7 %collective-permute-start.7 = (f32[128,256]{1,0:T(8,128)S(1)}, f32[128,256]{1,0:T(8,128)S(1)}, u32[]{:S(2)}, u32[]{:S(2)}) collective-permute-start(f32[128,256]{1,0:T(8,128)S(1)} %get-tuple-element.15), channel_id=1, source_target_pairs={{0,14},{2,0},{4,2},{6,4},{8,6},{10,8},{12,10},{14,12},{1,15},{3,1}... | collective-permute-start | bytes 393224 | tf_op jit(solution)/shard_map/ppermute | solution.py:165
  47.3 7.3 %collective-permute-start.3 = (f32[128,256]{1,0:T(8,128)S(1)}, f32[128,256]{1,0:T(8,128)S(1)}, u32[]{:S(2)}, u32[]{:S(2)}) collective-permute-start(f32[128,256]{1,0:T(8,128)S(1)} %get-tuple-element.16), channel_id=1, source_target_pairs={{0,2},{2,4},{4,6},{6,8},{8,10},{10,12},{12,14},{14,0},{1,3},{3,5},... | collective-permute-start | bytes 393224 | tf_op jit(solution)/shard_map/ppermute | solution.py:164
  51.3 7.7 %collective-permute-start.13 = (f32[128,256]{1,0:T(8,128)S(1)}, f32[128,256]{1,0:T(8,128)S(1)}, u32[]{:S(2)}, u32[]{:S(2)}) collective-permute-start(f32[128,256]{1,0:T(8,128)S(1)} %get-tuple-element.24), channel_id=1, source_target_pairs={{0,2},{2,4},{4,6},{6,8},{8,10},{10,12},{12,14},{14,0},{1,3},{3,5},... | collective-permute-start | bytes 393224 | tf_op jit(solution)/shard_map/ppermute | solution.py:164
  51.3 7.6 %collective-permute-start.17 = (f32[128,256]{1,0:T(8,128)S(1)}, f32[128,256]{1,0:T(8,128)S(1)}, u32[]{:S(2)}, u32[]{:S(2)}) collective-permute-start(f32[128,256]{1,0:T(8,128)S(1)} %get-tuple-element.23), channel_id=1, source_target_pairs={{0,14},{2,0},{4,2},{6,4},{8,6},{10,8},{12,10},{14,12},{1,15},{3,1}... | collective-permute-start | bytes 393224 | tf_op jit(solution)/shard_map/ppermute | solution.py:165
  55.6 6.3 %collective-permute-start.4 = (f32[128,256]{1,0:T(8,128)S(1)}, f32[128,256]{1,0:T(8,128)S(1)}, u32[]{:S(2)}, u32[]{:S(2)}) collective-permute-start(f32[128,256]{1,0:T(8,128)S(1)} %get-tuple-element.14), channel_id=1, source_target_pairs={{0,2},{2,4},{4,6},{6,8},{8,10},{10,12},{12,14},{14,0},{1,3},{3,5},... | collective-permute-start | bytes 393224 | tf_op jit(solution)/shard_map/ppermute | solution.py:164
  55.7 6.2 %collective-permute-start.8 = (f32[128,256]{1,0:T(8,128)S(1)}, f32[128,256]{1,0:T(8,128)S(1)}, u32[]{:S(2)}, u32[]{:S(2)}) collective-permute-start(f32[128,256]{1,0:T(8,128)S(1)} %get-tuple-element.13), channel_id=1, source_target_pairs={{0,14},{2,0},{4,2},{6,4},{8,6},{10,8},{12,10},{14,12},{1,15},{3,1}... | collective-permute-start | bytes 393224 | tf_op jit(solution)/shard_map/ppermute | solution.py:165
  62.8 1.6 %collective-permute-start.18 = (f32[2,128,256]{2,1,0:T(8,128)S(1)}, f32[2,128,256]{2,1,0:T(8,128)S(1)}, u32[]{:S(2)}, u32[]{:S(2)}) collective-permute-start(f32[2,128,256]{2,1,0:T(8,128)S(1)} %pad_maximum_fusion.mine_ref), channel_id=1, source_target_pairs={{0,1},{1,0},{2,3},{3,2},{4,5},{5,4},{6,7},{7,6},{8,9},{9,8},{10,11... | collective-permute-start | bytes 786440 | tf_op jit(solution)/shard_map/ppermute | solution.py:185
